TPU v7x, 32 devices: a whole 2x2x4 slice. The times are simulated.
32 devices in a mesh: grp: 2 (over x), frame: 8 (over z, y), row: 2 (over core).
Axes of the slice: x: 2, y: 2, z: 4, core: 2. Of those that a mesh axis runs over, the one named last changes fastest.
Arguments:
- latents: float32 [4, 8, 16, 32, 16], P('grp', 'frame', 'row'), parts along dimension 0, may hold values from -6 to 6
- target_noise: float32 [4, 8, 16, 32, 16], P('grp', 'frame', 'row'), parts along dimension 0, may hold values from -6 to 6
- timesteps: int32 [4], P('grp'), parts along dimension 0, may hold values from 0 to 999
- patch_weight: bfloat16 [16, 1152], replicated, may hold values from -1.5 to 1.5
- time_weight: bfloat16 [256, 1152], replicated, may hold values from -0.5 to 0.5
- spatial_project: bfloat16 [1152, 1728], replicated
- spatial_output: bfloat16 [576, 1152], replicated, may hold values from -0.75 to 0.75
- temporal_project: bfloat16 [1152, 1728], replicated
- temporal_output: bfloat16 [576, 1152], replicated, may hold values from -0.75 to 0.75
- final_weight: bfloat16 [1152, 16], replicated, may hold values from -0.1875 to 0.1875
Outputs:
- errors: float32 [4, 8, 16, 32], P('grp', 'frame', 'row'), parts along dimension 0
There are 2 independent parts, one for each index of `grp`. A program takes and returns all parts, laid end to end along the dimension named above; an argument that names none is the same for every part. Nothing has to cross between parts.
All inputs are finite; a program needn't handle non-finite values.
Results may differ from a plain program's by a relative error of at most 0.0045.
Values may be sent and summed in bfloat16 or wider, within the bound.
A program may use at most 128 MiB of HBM per device.

v0:
```python
import functools
import math

import jax
import jax.numpy as jnp
from jax import lax
from jax.experimental import pallas as pl
from jax.experimental.pallas import tpu as pltpu
from jax.sharding import PartitionSpec as P

HEAD_DIM = 72
HEADS = 8
STEPS = 1000
REACH = 2
HI = lax.Precision.HIGHEST
F32 = jnp.float32
MESH = pl.DeviceIdType.MESH


def noise_levels(timesteps):
    counter = jnp.arange(STEPS, dtype=F32)
    betas_all = 0.0001 + (0.02 - 0.0001) * counter / (STEPS - 1)
    log_keep = jnp.cumsum(jnp.log1p(-betas_all))
    selector = (jnp.arange(STEPS, dtype=jnp.int32)[None, :] == timesteps[:, None]).astype(F32)
    log_bar = jnp.dot(selector, log_keep, precision=HI)
    kept_share = jnp.exp(log_bar)
    return (jnp.sqrt(kept_share), jnp.sqrt(1.0 - kept_share))


def time_embed(timesteps, time_weight):
    halfway = time_weight.shape[0] // 2
    freqs_all = jnp.exp(-math.log(10000.0) * jnp.arange(halfway, dtype=F32) / halfway)
    angles = timesteps.astype(F32)[:, None] * freqs_all[None, :]
    features = jnp.concatenate([jnp.cos(angles), jnp.sin(angles)], axis=-1).astype(jnp.bfloat16)
    return jnp.dot(features, time_weight, preferred_element_type=F32)


def pieces(value, count):
    parts = []
    for _ in range(count):
        part = value.astype(jnp.bfloat16)
        parts.append(part)
        value = value - part.astype(F32)
    return parts


def wide_dot(value, weight, count=2):
    rows = value.shape[0]
    out = jnp.dot(jnp.concatenate(pieces(value, count), axis=0), weight, preferred_element_type=F32)
    return sum(out[i * rows : (i + 1) * rows] for i in range(count))


def centre(value):
    return value - jnp.mean(value, axis=-1, keepdims=True)


def local(
    latents,
    target_noise,
    timesteps,
    patch_weight,
    time_weight,
    spatial_project,
    spatial_output,
    temporal_project,
    temporal_output,
    final_weight,
):
    batches, frames_l, rows_l, cols, ch = latents.shape
    peers, halves = lax.axis_size("frame"), lax.axis_size("row")
    fi, gi = lax.axis_index("frame"), lax.axis_index("row")
    frames, rows = frames_l * peers, rows_l * halves
    places = rows_l * cols // peers
    q_rows, q_cols = max(1, places // cols), min(cols, places)
    width = patch_weight.shape[1]
    inner = spatial_output.shape[0]
    scale = 1.0 / math.sqrt(HEAD_DIM)

    signal, spread = noise_levels(timesteps)
    noisy = (
        signal[:, None, None, None, None] * latents
        + spread[:, None, None, None, None] * target_noise
    ).astype(jnp.bfloat16)
    time_vector = time_embed(timesteps, time_weight)

    whole = lax.all_gather(
        noisy.reshape(batches, frames_l, rows_l, cols * ch), ("frame", "row"), axis=0, tiled=False
    )
    whole = whole.reshape(peers, halves, batches, frames_l, rows_l, cols * ch)
    whole = whole.transpose(2, 0, 3, 1, 4, 5).reshape(batches, frames, rows, cols * ch)
    target = lax.all_to_all(
        target_noise.reshape(batches, frames_l, peers, places * ch),
        "frame",
        split_axis=2,
        concat_axis=1,
        tiled=True,
    ).reshape(batches * frames * places, ch)

    first = gi * rows_l + (fi * places) // cols
    column = (fi * places) % cols
    k_rows = q_rows + 2 * REACH
    padded = jnp.pad(whole, ((0, 0), (0, 0), (REACH, REACH), (0, 0)))
    near = lax.dynamic_slice_in_dim(padded, first, k_rows, axis=2).reshape(
        batches, frames, k_rows, cols, ch
    )
    own = lax.dynamic_slice_in_dim(near[:, :, REACH : REACH + q_rows], column, q_cols, axis=3)

    base = jnp.concatenate([patch_weight.astype(F32), time_vector], axis=0)
    base_c = centre(base)
    feats = base.shape[0]
    spatial = wide_dot(base_c, spatial_project, 3).reshape(feats, 3, HEADS, HEAD_DIM)
    mixer = jnp.einsum("ahe,bhe->hab", spatial[:, 0], spatial[:, 1], precision=HI) * scale
    out_heads = spatial_output.reshape(HEADS, HEAD_DIM, width).astype(F32)
    carried = jnp.einsum("ahe,hed->had", spatial[:, 2], out_heads, precision=HI)
    full_c = jnp.concatenate([base_c, centre(carried).reshape(HEADS * feats, width)], axis=0)
    temporal = wide_dot(full_c, temporal_project, 2)

    def lifted(tokens):
        mark = jnp.broadcast_to(
            jnp.eye(batches, dtype=F32)[:, None, None, None, :], tokens.shape[:-1] + (batches,)
        )
        return jnp.concatenate([tokens.astype(F32), mark], axis=-1)

    def scaled(tokens):
        stream = jnp.einsum("bfrca,ad->bfrcd", tokens, base_c, precision=HI)
        return tokens * lax.rsqrt(jnp.mean(stream * stream, axis=-1, keepdims=True) + 1e-06)

    near_l, own_l = lifted(near), lifted(own)
    keys = scaled(near_l).reshape(batches, frames, k_rows * cols, feats)
    query = scaled(own_l).reshape(batches, frames, places, feats)
    query = jnp.einsum("bfqa,hac->bfhqc", query, mixer, precision=HI)
    scores = jnp.einsum("bfhqc,bfkc->bfhqk", query, keys, precision=HI)
    key_row = jnp.arange(k_rows * cols, dtype=jnp.int32) // cols
    query_row = jnp.arange(places, dtype=jnp.int32) // q_cols
    off = key_row[None, :] - query_row[:, None]
    there = first + key_row - REACH
    inside = ((off >= 0) & (off <= 2 * REACH)) & ((there >= 0) & (there < rows))[None, :]
    scores = jnp.where(inside, scores, -1e30)
    exponent = jnp.exp(scores - jnp.max(scores, axis=-1, keepdims=True))
    weights = exponent / jnp.sum(exponent, axis=-1, keepdims=True)
    mixed = jnp.einsum("bfhqk,bfkc->bfqhc", weights, keys, precision=HI)
    tokens = batches * frames * places
    state = jnp.concatenate(
        [own_l.reshape(tokens, feats), mixed.reshape(tokens, HEADS * feats)], axis=-1
    )

    stream = jnp.dot(state, full_c, precision=HI)
    share = lax.rsqrt(jnp.mean(stream * stream, axis=-1, keepdims=True) + 1e-06)
    projected = (jnp.dot(state, temporal, precision=HI) * share).astype(jnp.bfloat16)
    shaped = projected.reshape(batches, frames, places, 3, HEADS, HEAD_DIM)
    scores = (
        jnp.einsum(
            "bfphe,bgphe->bphfg", shaped[:, :, :, 0], shaped[:, :, :, 1], preferred_element_type=F32
        )
        * scale
    )
    exponent = jnp.exp(scores - jnp.max(scores, axis=-1, keepdims=True))
    weights = (exponent / jnp.sum(exponent, axis=-1, keepdims=True)).astype(jnp.bfloat16)
    mixed = (
        jnp.einsum("bphfg,bgphe->bfphe", weights, shaped[:, :, :, 2], preferred_element_type=F32)
        .astype(jnp.bfloat16)
        .reshape(tokens, inner)
    )
    stream = stream + jnp.dot(mixed, temporal_output, preferred_element_type=F32)
    stream = centre(stream)
    share = lax.rsqrt(jnp.mean(stream * stream, axis=-1, keepdims=True) + 1e-06)
    predicted = jnp.dot(
        (stream * share).astype(jnp.bfloat16), final_weight, preferred_element_type=F32
    )
    gap = predicted - target
    errors = jnp.mean(gap * gap, axis=-1).reshape(batches, frames, places)
    errors = lax.all_to_all(errors, "frame", split_axis=1, concat_axis=2, tiled=True)
    return errors.reshape(batches, frames_l, rows_l, cols)


def split2(value):
    high = value.astype(jnp.bfloat16)
    return high, (value - high.astype(F32)).astype(jnp.bfloat16)


def dot(a, b, axes=((1,), (0,)), precision=None):
    return lax.dot_general(a, b, (axes, ((), ())), precision=precision, preferred_element_type=F32)


NT = ((1,), (1,))


def fused_kernel(
    peers,
    halves,
    batches,
    cols,
    x_ref,
    target_ref,
    base_ref,
    final_ref,
    sp_hbm,
    so_hbm,
    tp_hbm,
    to_hbm,
    out_ref,
    sp,
    so,
    tp,
    to,
    w_sem,
    near,
    goal,
    err_out,
    err_in,
    mall,
    full_hi,
    full_lo,
    gram,
    gt_hi,
    gt_lo,
    state,
    qkv,
    mixed_t,
    x_send,
    x_recv,
    h_send,
    h_recv,
    t_send,
    t_recv,
    e_send,
    e_recv,
):
    rows_l, ch, lanes = x_ref.shape
    per = batches * cols
    pair = lanes // per
    width = base_ref.shape[1]
    inner = so.shape[0]
    feats = base_ref.shape[0]
    window = 2 * REACH + 1
    fi, gi = lax.axis_index("frame"), lax.axis_index("row")
    weight_copies = [
        pltpu.make_async_copy(src, dst, w_sem.at[i])
        for i, (src, dst) in enumerate(((sp_hbm, sp), (so_hbm, so), (tp_hbm, tp), (to_hbm, to)))
    ]
    for copy in weight_copies:
        copy.start()

    barrier = pltpu.get_barrier_semaphore()
    for df in range(peers):
        for dg in range(halves):
            if df or dg:
                pl.semaphore_signal(
                    barrier,
                    inc=1,
                    device_id={
                        "frame": lax.rem(fi + df, peers),
                        "row": lax.rem(gi + dg, halves),
                    },
                    device_id_type=MESH,
                )
    pl.semaphore_wait(barrier, peers * halves - 1)

    def start_of(place):
        return jnp.clip(place - REACH, 0, rows_l - window)

    def x_copy(peer):
        return pltpu.make_async_remote_copy(
            src_ref=x_ref.at[pl.ds(start_of(peer), window)],
            dst_ref=near.at[fi, pl.ds(0, window)],
            send_sem=x_send.at[peer],
            recv_sem=x_recv.at[fi],
            device_id={"frame": peer, "row": gi},
            device_id_type=MESH,
        )

    def t_copy(peer):
        return pltpu.make_async_remote_copy(
            src_ref=target_ref.at[peer],
            dst_ref=goal.at[fi],
            send_sem=t_send.at[peer],
            recv_sem=t_recv.at[fi],
            device_id={"frame": peer, "row": gi},
            device_id_type=MESH,
        )

    def halo_copy(slot, peer, half, first):
        return pltpu.make_async_remote_copy(
            src_ref=x_ref.at[pl.ds(first, REACH)],
            dst_ref=near.at[fi, pl.ds(window, REACH)],
            send_sem=h_send.at[slot],
            recv_sem=h_recv.at[fi],
            device_id={"frame": peer, "row": half},
            device_id_type=MESH,
        )

    def halos(action):
        for i in range(REACH):

            @pl.when(gi < halves - 1)
            def _():
                action(halo_copy(i, i, gi + 1, rows_l - REACH))

            @pl.when(gi > 0)
            def _():
                action(halo_copy(REACH + i, peers - REACH + i, gi - 1, 0))

    halos(lambda copy: copy.start())
    for k in range(1, peers):
        x_copy(lax.rem(fi + k, peers)).start()
    for k in range(1, peers):
        t_copy(lax.rem(fi + k, peers)).start()
    near[fi, 0:window] = x_ref[pl.ds(start_of(fi), window)]
    goal[fi] = target_ref[fi]
    takes_halo = ((fi < REACH) & (gi > 0)) | ((fi >= peers - REACH) & (gi < halves - 1))

    @pl.when(jnp.logical_not(takes_halo))
    def _():
        near[:, window:] = jnp.zeros((peers, REACH, ch, lanes), near.dtype)

    base = base_ref[...]
    base_c = base - jnp.mean(base, axis=-1, keepdims=True)
    b1, b2 = split2(base_c)
    b3 = (base_c - b1.astype(F32) - b2.astype(F32)).astype(jnp.bfloat16)
    weight_copies[0].wait()
    wide = dot(jnp.concatenate([b1, b2, b3], axis=0), sp[...])
    spatial = wide[:feats] + wide[feats : 2 * feats] + wide[2 * feats :]
    sq, sk, sv = (spatial[:, i * inner : (i + 1) * inner] for i in range(3))
    owner = lax.broadcasted_iota(jnp.int32, (feats, inner), 1) // HEAD_DIM

    def by_head(value):
        return jnp.concatenate(
            [jnp.where(owner == h, value, 0.0) for h in range(HEADS)], axis=0
        )

    sk3 = jnp.concatenate([sk] * 3 + [jnp.zeros((128 - 3 * feats, inner), F32)], axis=0)
    mixer = dot(by_head(sq), sk3, NT, HI) * (1.0 / math.sqrt(HEAD_DIM))
    for h in range(HEADS):
        mall[:, h * 128 : (h + 1) * 128] = mixer[h * feats : (h + 1) * feats]
    v1, v2 = split2(by_head(sv))
    weight_copies[1].wait()
    carried = dot(v1, so[...]) + dot(v2, so[...])
    carried = carried - jnp.mean(carried, axis=-1, keepdims=True)
    rest = state.shape[0] - feats * (HEADS + 1)
    full = jnp.concatenate([base_c, carried, jnp.zeros((rest, width), F32)], axis=0)
    f1, f2 = split2(full)
    full_hi[...] = f1
    full_lo[...] = f2
    gram[...] = (dot(f1, f1, NT) + dot(f1, f2, NT) + dot(f2, f1, NT)) * (1.0 / width)
    weight_copies[2].wait()
    g1, g2 = split2((dot(f1, tp[...]) + dot(f2, tp[...])).T)
    gt_hi[...] = g1
    gt_lo[...] = g2
    small = dot(base_c, base_c, NT, HI) * (1.0 / width)

    for k in range(1, peers):
        x_copy(lax.rem(fi + k, peers)).wait_send()
        pltpu.make_async_remote_copy(
            src_ref=x_ref.at[pl.ds(0, window)],
            dst_ref=near.at[lax.rem(fi + k, peers), pl.ds(0, window)],
            send_sem=x_send.at[fi],
            recv_sem=x_recv.at[lax.rem(fi + k, peers)],
            device_id={"frame": lax.rem(fi + k, peers), "row": gi},
            device_id_type=MESH,
        ).wait_recv()
    halos(lambda copy: copy.wait_send())

    @pl.when(takes_halo)
    def _():
        for k in range(peers):
            pltpu.make_async_remote_copy(
                src_ref=x_ref.at[pl.ds(0, REACH)],
                dst_ref=near.at[k, pl.ds(window, REACH)],
                send_sem=h_send.at[0],
                recv_sem=h_recv.at[k],
                device_id={"frame": k, "row": lax.rem(gi + 1, halves)},
                device_id_type=MESH,
            ).wait_recv()

    mark = (
        lax.broadcasted_iota(jnp.int32, (feats - ch, lanes), 1) // cols
        == lax.broadcasted_iota(jnp.int32, (feats - ch, lanes), 0)
    ).astype(F32)
    spots, biases = [], []
    for d in range(-REACH, REACH + 1):
        lr = fi + d
        spots.append(
            jnp.where(
                lr < 0,
                window + lr + REACH,
                jnp.where(lr >= rows_l, window + lr - rows_l, lr - start_of(fi)),
            )
        )
        there = gi * rows_l + lr
        biases.append(jnp.where((there >= 0) & (there < rows_l * halves), 0.0, -1e30).astype(F32))

    tiles_of_u = []
    for f in range(peers):
        lifted = jnp.concatenate(
            [
                jnp.concatenate([near[f, spot].astype(F32), mark], axis=0)
                for spot in spots
            ],
            axis=1,
        )
        var = jnp.sum(lifted * dot(small, lifted, precision=HI), axis=0, keepdims=True)
        y = lifted * lax.rsqrt(jnp.maximum(var, 0.0) + 1e-06)
        high = y.astype(jnp.bfloat16).astype(F32)
        keys3 = jnp.concatenate(
            [high, y - high, high, jnp.zeros((128 - 3 * feats, window * lanes), F32)], axis=0
        )
        keys3 = [keys3[:, i * lanes : (i + 1) * lanes].T for i in range(window)]
        own = y[:, REACH * lanes : (REACH + 1) * lanes].T[:per]
        ask = dot(own, mall[...], precision=HI)
        lead = ask.astype(jnp.bfloat16).astype(F32)
        lane = lax.broadcasted_iota(jnp.int32, ask.shape, 1) % 128
        ask3 = jnp.where(lane < 2 * feats, lead, ask - lead).astype(jnp.bfloat16)
        state[0:feats, f * per : (f + 1) * per] = lifted[
            :, REACH * lanes : REACH * lanes + per
        ]
        for b in range(batches):
            cut = slice(b * cols, (b + 1) * cols)
            k3 = jnp.concatenate([k[cut] for k in keys3], axis=0).astype(jnp.bfloat16)
            q3 = jnp.concatenate(
                [ask3[cut, h * 128 : (h + 1) * 128] for h in range(HEADS)], axis=0
            )
            scores = dot(k3, q3, NT)
            scores = jnp.concatenate(
                [scores[i * cols : (i + 1) * cols] + biases[i] for i in range(window)], axis=0
            )
            weight = jnp.exp(scores - jnp.max(scores, axis=0, keepdims=True))
            weight = weight * (1.0 / jnp.sum(weight, axis=0, keepdims=True))
            both = dot(k3, weight.astype(jnp.bfloat16), ((0,), (0,)))
            tiles_of_u.append(both[:feats] + both[feats : 2 * feats])
    for h in range(HEADS):
        state[feats * (h + 1) : feats * (h + 2), :] = jnp.concatenate(
            [u[:, h * cols : (h + 1) * cols] for u in tiles_of_u], axis=1
        )
    state[feats * (HEADS + 1) :, :] = jnp.zeros((rest, state.shape[1]), F32)

    z = state[...]
    z1, z2 = split2(z)
    var = jnp.sum(z * (dot(gram[...], z, precision=HI)), axis=0, keepdims=True)
    share = lax.rsqrt(jnp.maximum(var, 0.0) + 1e-06)
    qkv[...] = (dot(gt_hi[...], z1) + dot(gt_hi[...], z2) + dot(gt_lo[...], z1)) * share
    tiles = peers // pair
    scale = 1.0 / math.sqrt(HEAD_DIM)

    def tile_of(part, h, t):
        top = part * inner + h * HEAD_DIM
        return qkv[top : top + HEAD_DIM, t * lanes : (t + 1) * lanes]

    def turned(value, s):
        return pltpu.roll(value, s * per, 1) if s else value

    for h in range(HEADS):
        ks = [turned(tile_of(1, h, t), s) for t in range(tiles) for s in range(pair)]
        vs = [turned(tile_of(2, h, t), s) for t in range(tiles) for s in range(pair)]
        for p in range(tiles):
            q = tile_of(0, h, p) * scale
            logits = [jnp.sum(q * k, axis=0, keepdims=True) for k in ks]
            top = functools.reduce(jnp.maximum, logits)
            exps = [jnp.exp(s - top) for s in logits]
            total = 1.0 / functools.reduce(jnp.add, exps)
            acc = functools.reduce(
                jnp.add, [(e * total) * v for e, v in zip(exps, vs)]
            )
            mixed_t[h * HEAD_DIM : (h + 1) * HEAD_DIM, p * lanes : (p + 1) * lanes] = acc

    zt = z.T
    zt1, zt2 = split2(zt)
    weight_copies[3].wait()
    stream = dot(zt1, full_hi[...]) + dot(zt2, full_hi[...]) + dot(zt1, full_lo[...])
    stream = stream + dot(mixed_t[...].T.astype(jnp.bfloat16), to[...])
    stream = stream - jnp.mean(stream, axis=-1, keepdims=True)
    share = lax.rsqrt(jnp.mean(stream * stream, axis=-1, keepdims=True) + 1e-06)
    predicted = dot(final_ref[...], (stream * share).astype(jnp.bfloat16), NT)

    for k in range(1, peers):
        t_copy(lax.rem(fi + k, peers)).wait_send()
        pltpu.make_async_remote_copy(
            src_ref=target_ref.at[0],
            dst_ref=goal.at[lax.rem(fi + k, peers)],
            send_sem=t_send.at[fi],
            recv_sem=t_recv.at[lax.rem(fi + k, peers)],
            device_id={"frame": lax.rem(fi + k, peers), "row": gi},
            device_id_type=MESH,
        ).wait_recv()
    aim = jnp.concatenate([goal[f][:, :per] for f in range(peers)], axis=1)
    gap = predicted - aim
    errors = jnp.mean(gap * gap, axis=0, keepdims=True)
    for t in range(tiles):
        err_out[t] = jnp.broadcast_to(errors[:, t * lanes : (t + 1) * lanes], (8, lanes))

    def e_copy(peer, source, other):
        return pltpu.make_async_remote_copy(
            src_ref=err_out.at[peer // pair],
            dst_ref=err_in.at[source],
            send_sem=e_send.at[peer],
            recv_sem=e_recv.at[source],
            device_id={"frame": other, "row": gi},
            device_id_type=MESH,
        )

    for k in range(1, peers):
        e_copy(lax.rem(fi + k, peers), fi, lax.rem(fi + k, peers)).start()
    err_in[fi] = err_out[fi // pair]
    for k in range(1, peers):
        other = lax.rem(fi + k, peers)
        e_copy(other, fi, other).wait_send()
        e_copy(fi, other, other).wait_recv()
    got = jnp.concatenate([err_in[k, 0:1] for k in range(peers)], axis=0)
    result = got[:, :per]
    for s in range(1, pair):
        result = jnp.where(lax.rem(fi, pair) == s, got[:, s * per : (s + 1) * per], result)
    out_ref[...] = result


def fused(
    latents,
    target_noise,
    timesteps,
    patch_weight,
    time_weight,
    spatial_project,
    spatial_output,
    temporal_project,
    temporal_output,
    final_weight,
):
    batches, _, rows_l, cols, ch = latents.shape
    peers, halves = lax.axis_size("frame"), lax.axis_size("row")
    width, inner = patch_weight.shape[1], spatial_output.shape[0]
    per, lanes = batches * cols, 128
    signal, spread = noise_levels(timesteps)
    noisy = (
        signal[:, None, None, None, None] * latents
        + spread[:, None, None, None, None] * target_noise
    ).astype(jnp.bfloat16)

    def channel_major(value):
        value = value[:, 0].transpose(1, 3, 0, 2).reshape(rows_l, ch, per)
        return jnp.pad(value, ((0, 0), (0, 0), (0, lanes - per)))

    feats = -(-(ch + batches) // 8) * 8
    time_vector = time_embed(timesteps, time_weight)
    base = jnp.concatenate(
        [
            patch_weight.astype(F32),
            time_vector,
            jnp.zeros((feats - ch - batches, width), F32),
        ],
        axis=0,
    )
    tokens = peers * per
    depth = -(-(feats * (HEADS + 1)) // 128) * 128
    bf16 = jnp.bfloat16
    vmem, anywhere = pl.BlockSpec(memory_space=pltpu.VMEM), pl.BlockSpec(memory_space=pl.ANY)
    sems = pltpu.SemaphoreType.DMA
    out = pl.pallas_call(
        functools.partial(fused_kernel, peers, halves, batches, cols),
        out_shape=jax.ShapeDtypeStruct((rows_l, per), F32),
        in_specs=[vmem] * 4 + [anywhere] * 4,
        out_specs=vmem,
        scratch_shapes=[
            pltpu.VMEM(spatial_project.shape, bf16),
            pltpu.VMEM(spatial_output.shape, bf16),
            pltpu.VMEM(temporal_project.shape, bf16),
            pltpu.VMEM(temporal_output.shape, bf16),
            sems((4,)),
            pltpu.VMEM((peers, 3 * REACH + 1, ch, lanes), bf16),
            pltpu.VMEM((peers, ch, lanes), F32),
            pltpu.VMEM((tokens // lanes, 8, lanes), F32),
            pltpu.VMEM((peers, 8, lanes), F32),
            pltpu.VMEM((feats, HEADS * 128), F32),
            pltpu.VMEM((depth, width), bf16),
            pltpu.VMEM((depth, width), bf16),
            pltpu.VMEM((depth, depth), F32),
            pltpu.VMEM((3 * inner, depth), bf16),
            pltpu.VMEM((3 * inner, depth), bf16),
            pltpu.VMEM((depth, tokens), F32),
            pltpu.VMEM((3 * inner, tokens), F32),
            pltpu.VMEM((inner, tokens), F32),
            sems((peers,)),
            sems((peers,)),
            sems((2 * REACH,)),
            sems((peers,)),
            sems((peers,)),
            sems((peers,)),
            sems((peers,)),
            sems((peers,)),
        ],
        compiler_params=pltpu.CompilerParams(
            collective_id=0, has_side_effects=True, vmem_limit_bytes=56 * 1024 * 1024
        ),
        cost_estimate=pl.CostEstimate(
            flops=4 * 10**9, bytes_accessed=11 * 10**6, transcendentals=10**6
        ),
    )(
        channel_major(noisy),
        channel_major(target_noise),
        base,
        final_weight.T,
        spatial_project,
        spatial_output,
        temporal_project,
        temporal_output,
    )
    return out.reshape(rows_l, batches, cols).transpose(1, 0, 2)[:, None]


def fits(latents):
    batches, frames_l, rows_l, cols, ch = latents.shape
    per = batches * cols
    return (
        frames_l == 1
        and rows_l == lax.axis_size("frame")
        and rows_l >= 3 * REACH
        and 128 % per == 0
        and (rows_l * per) % 128 == 0
        and ch % 16 == 0
        and 3 * (ch + batches) <= 96
    )


def choose(latents, target_noise, timesteps, *weights):
    plan = fused if fits(latents) else local
    return plan(latents, target_noise, timesteps, *weights)


def solution(mesh):
    data = P("grp", "frame", "row", None, None)
    return jax.shard_map(
        choose,
        mesh=mesh,
        in_specs=(data, data, P("grp")) + (P(),) * 7,
        out_specs=P("grp", "frame", "row", None),
        check_vma=False,
    )
```

profile of v0, /device:TPU:0, one launch (start us, length us, event | category | flops | bytes accessed | tf_op | source)
XLA Modules:
  0.0 56.4 jit_solution(8929978844509149388)
XLA Ops:
  0.0 0.0 copy-start
  0.0 0.7 %convert_element_type.17 = f32[2]{0:T(128)S(1)} convert(s32[2]{0:T(128)} %param.12) | non-fusion elementwise | flops 2 | bytes 16 | tf_op jit(solution)/shard_map/convert_element_type | solution.py:33
  0.7 0.1 pad.16.clone
  0.8 0.1 fusion.5
  1.0 0.3 reduce-window.9
  1.2 0.1 slice.10
  1.3 0.1 slice_reduce_fusion
  1.5 0.1 add_bitcast_fusion
  1.5 0.9 %fusion.12 = (f32[2]{0:T(128)S(1)}, f32[2]{0:T(128)S(1)}) fusion(f32[1000,1]{0,1:T(1,128)S(1)} %bitcast.26, s32[2]{0:T(128)} %param.12), kind=kOutput, calls=%fused_computation.24 | convolution fusion | flops 26002 | bytes 4024 | tf_op jit(solution)/shard_map/dot_general | solution.py:25
  2.4 0.0 copy-done
  2.4 0.2 fusion.7
  2.6 1.1 %fusion.1 = bf16[8,16,2,32]{3,1,0,2:T(8,128)(2,1)S(1)} fusion(f32[2,1,8,32,16]{3,4,2,1,0:T(8,128)} %param.11, f32[2,1,8,32,16]{3,4,2,1,0:T(8,128)} %param.10, f32[2]{0:T(128)S(1)} %get-tuple-element.8, f32[2]{0:T(128)S(1)} %get-tuple-element.7), kind=kLoop, calls=%fused_computation.4 | loop fusion | flops 32768 | bytes 81936 | tf_op jit(solution)/shard_map/transpose | solution.py:537
  3.7 0.1 copy.16
  3.8 0.1 reshape.38
  3.9 0.6 %pad.12.x_ref = bf16[8,16,128]{2,1,0:T(8,128)(2,1)} pad(bf16[8,16,64]{2,1,0:T(8,128)(2,1)S(1)} %reshape.38, bf16[]{:T(256)} %constant.21.clone.1), padding=0_0x0_0x0_64 | pad | bytes 49154 | tf_op jit(solution)/shard_map/jit(_pad)/pad | solution.py:538
  4.5 0.8 %convert_element_type.16 = f32[16,1152]{1,0:T(8,128)S(1)} convert(bf16[16,1152]{1,0:T(8,128)(2,1)} %param.13) | non-fusion elementwise | flops 18432 | bytes 110592 | tf_op jit(solution)/shard_map/convert_element_type | solution.py:544
  5.3 0.7 %maximum_maximum_fusion.base_ref = f32[24,1152]{1,0:T(8,128)} fusion(f32[2,1152]{1,0:T(2,128)S(1)} %fusion.7, f32[16,1152]{1,0:T(8,128)S(1)} %convert_element_type.16, f32[24]{0:T(128)S(1)} %pad.16.clone), kind=kLoop, calls=%fused_computation.3 | loop fusion | flops 55296 | bytes 193632 | tf_op jit(solution)/shard_map/concatenate | solution.py:542
  6.0 1.0 %copy.17 = f32[8,16,2,32]{3,2,1,0:T(2,128)S(1)} copy(f32[8,16,2,32]{3,1,0,2:T(8,128)} %bitcast.25) | data formatting | bytes 65536 | tf_op jit(solution)/shard_map/transpose | solution.py:537
  7.0 0.1 reshape.39
  7.1 0.6 %pad.13.target_ref = f32[8,16,128]{2,1,0:T(8,128)} pad(f32[8,16,64]{2,1,0:T(8,128)S(1)} %reshape.39, f32[]{:T(128)} %constant.19.clone.1), padding=0_0x0_0x0_64 | pad | bytes 98308 | tf_op jit(solution)/shard_map/jit(_pad)/pad | solution.py:538
  7.8 6.4 %copy.18.sp_hbm = bf16[1152,1728]{1,0:T(8,128)(2,1)} copy(bf16[1152,1728]{0,1:T(8,128)(2,1)} %param.15) | data formatting | bytes 7962624 | tf_op args[5]
  14.2 6.5 %copy.19.tp_hbm = bf16[1152,1728]{1,0:T(8,128)(2,1)} copy(bf16[1152,1728]{0,1:T(8,128)(2,1)} %param.17) | data formatting | bytes 7962624 | tf_op args[7]
  20.7 34.3 %shard_map.100 = f32[8,64]{1,0:T(8,128)} custom-call(bf16[8,16,128]{2,1,0:T(8,128)(2,1)} %pad.12.x_ref, f32[8,16,128]{2,1,0:T(8,128)} %pad.13.target_ref, f32[24,1152]{1,0:T(8,128)} %maximum_maximum_fusion.base_ref, bf16[16,1152]{1,0:T(8,128)(2,1)} %bitcast.27, bf16[1152,1728]{1,0:T(8,128)(2,1)} %copy.18.sp_hbm, bf16[576,1152]{1,0:T(8,128)(2,1)} %so_hbm.1, ...), custom_call_target="tpu_custom_call" | custom-call | flops 4000000000 | bytes 11000000 | tf_op jit(solution)/shard_map/pallas_call | solution.py:555
  55.0 0.8 %reshape.40 = f32[8,2,32]{2,1,0:T(2,128)S(1)} reshape(f32[8,64]{1,0:T(8,128)} %shard_map.100) | data formatting | bytes 4096 | tf_op jit(solution)/shard_map/reshape | solution.py:604
  55.8 0.6 %copy.22 = f32[8,2,32]{2,0,1:T(8,128)} copy(f32[8,2,32]{2,1,0:T(2,128)S(1)} %reshape.40) | data formatting | bytes 4096 | tf_op jit(solution)/shard_map/reshape | solution.py:604
  (5 shorter events, 0.1 us)
Async XLA Ops:
  0.0 2.4 %copy-start = (bf16[256,1152]{1,0:T(8,128)(2,1)S(1)}, bf16[256,1152]{1,0:T(8,128)(2,1)}, u32[]{:S(2)}) copy-start(bf16[256,1152]{1,0:T(8,128)(2,1)} %param.14) | copy-start | bytes 1769476
where the time goes:
time: 56.9 us; the launch traced here: 56.4 us
  Pallas kernels  34.3 us (60%)
  local copies, waits for them, and re-layouts  17.1 us (30%)
  other arithmetic  3.81 us (7%)
  matrix products  1.07 us (2%)
    pallas_call x1, Pallas kernels, fused(): pl.pallas_call(functools.partial(fused_kernel, peers, halves, batches, co...  34.3 us
    unnamed x4, local copies, waits for them, and re-layouts  12.9 us
    reshape x2, local copies, waits for them, and re-layouts, fused(): return out.reshape(rows_l, batches, cols).transpose(1, 0, 2)[:, None]  1.36 us
    pad x2, local copies, waits for them, and re-layouts, channel_major(): return jnp.pad(value, ((0, 0), (0, 0), (0, lanes - per)))  1.25 us

commit v1 on v0

--- a/solution.py
+++ b/solution.py
@@ -173,11 +173,6 @@
     return errors.reshape(batches, frames_l, rows_l, cols)
 
 
-def split2(value):
-    high = value.astype(jnp.bfloat16)
-    return high, (value - high.astype(F32)).astype(jnp.bfloat16)
-
-
 def dot(a, b, axes=((1,), (0,)), precision=None):
     return lax.dot_general(a, b, (axes, ((), ())), precision=precision, preferred_element_type=F32)
 
@@ -188,33 +183,33 @@
 def fused_kernel(
     peers,
     halves,
-    batches,
-    cols,
-    x_ref,
-    target_ref,
-    base_ref,
+    times_ref,
+    lat_ref,
+    noise_ref,
+    patch_ref,
     final_ref,
+    tw_hbm,
     sp_hbm,
     so_hbm,
     tp_hbm,
     to_hbm,
     out_ref,
+    tw,
     sp,
     so,
     tp,
     to,
     w_sem,
+    x_ref,
+    target_ref,
     near,
     goal,
     err_out,
     err_in,
-    mall,
-    full_hi,
-    full_lo,
-    gram,
-    gt_hi,
-    gt_lo,
+    full,
+    gt,
     state,
+    stream1,
     qkv,
     mixed_t,
     x_send,
@@ -226,17 +221,19 @@
     e_send,
     e_recv,
 ):
-    rows_l, ch, lanes = x_ref.shape
+    batches, _, rows_l, ch, cols = lat_ref.shape
+    lanes = x_ref.shape[-1]
     per = batches * cols
     pair = lanes // per
-    width = base_ref.shape[1]
+    width = patch_ref.shape[1]
     inner = so.shape[0]
-    feats = base_ref.shape[0]
+    feats = ch + 8
+    depth = full.shape[0]
     window = 2 * REACH + 1
     fi, gi = lax.axis_index("frame"), lax.axis_index("row")
+    pairs = ((tw_hbm, tw), (sp_hbm, sp), (so_hbm, so), (tp_hbm, tp), (to_hbm, to))
     weight_copies = [
-        pltpu.make_async_copy(src, dst, w_sem.at[i])
-        for i, (src, dst) in enumerate(((sp_hbm, sp), (so_hbm, so), (tp_hbm, tp), (to_hbm, to)))
+        pltpu.make_async_copy(src, dst, w_sem.at[i]) for i, (src, dst) in enumerate(pairs)
     ]
     for copy in weight_copies:
         copy.start()
@@ -254,6 +251,23 @@
                     },
                     device_id_type=MESH,
                 )
+
+    index = 128 * lax.broadcasted_iota(jnp.int32, (8, 128), 0) + lax.broadcasted_iota(
+        jnp.int32, (8, 128), 1
+    )
+    logs = jnp.log1p(-(0.0001 + (0.02 - 0.0001) * index.astype(F32) / (STEPS - 1)))
+    logs = jnp.where(index < STEPS, logs, 0.0)
+    noisy = []
+    for b in range(batches):
+        kept = jnp.where(index <= times_ref[b], logs, 0.0)
+        kept = jnp.exp(jnp.sum(jnp.sum(kept, axis=1, keepdims=True), axis=0, keepdims=True))
+        signal, spread = jnp.sqrt(kept)[None], jnp.sqrt(1.0 - kept)[None]
+        noisy.append(signal * lat_ref[b, 0] + spread * noise_ref[b, 0])
+    blank = [jnp.zeros((rows_l, ch, lanes - per), F32)] if lanes > per else []
+    x_ref[...] = jnp.concatenate(noisy + blank, axis=2).astype(jnp.bfloat16)
+    target_ref[...] = jnp.concatenate(
+        [noise_ref[b, 0] for b in range(batches)] + blank, axis=2
+    )
     pl.semaphore_wait(barrier, peers * halves - 1)
 
     def start_of(place):
@@ -300,9 +314,9 @@
             def _():
                 action(halo_copy(REACH + i, peers - REACH + i, gi - 1, 0))
 
-    halos(lambda copy: copy.start())
     for k in range(1, peers):
         x_copy(lax.rem(fi + k, peers)).start()
+    halos(lambda copy: copy.start())
     for k in range(1, peers):
         t_copy(lax.rem(fi + k, peers)).start()
     near[fi, 0:window] = x_ref[pl.ds(start_of(fi), window)]
@@ -313,12 +327,23 @@
     def _():
         near[:, window:] = jnp.zeros((peers, REACH, ch, lanes), near.dtype)
 
-    base = base_ref[...]
+    halfway = tw.shape[0] // 2
+    row = lax.broadcasted_iota(jnp.int32, (8, halfway), 0)
+    place = lax.broadcasted_iota(jnp.int32, (8, halfway), 1)
+    when = jnp.zeros((8, halfway), jnp.int32)
+    for b in range(batches):
+        when = jnp.where(row == b, times_ref[b], when)
+    angles = when.astype(F32) * jnp.exp(-math.log(10000.0) * place.astype(F32) / halfway)
+    used = row < batches
+    features = jnp.concatenate(
+        [jnp.where(used, jnp.cos(angles), 0.0), jnp.where(used, jnp.sin(angles), 0.0)], axis=1
+    ).astype(jnp.bfloat16)
+    weight_copies[0].wait()
+    base = jnp.concatenate([patch_ref[...].astype(F32), dot(features, tw[...])], axis=0)
     base_c = base - jnp.mean(base, axis=-1, keepdims=True)
-    b1, b2 = split2(base_c)
-    b3 = (base_c - b1.astype(F32) - b2.astype(F32)).astype(jnp.bfloat16)
-    weight_copies[0].wait()
-    wide = dot(jnp.concatenate([b1, b2, b3], axis=0), sp[...])
+    b1, b2, b3 = pieces(base_c, 3)
+    weight_copies[1].wait()
+    wide = dot(jnp.concatenate([b1, b2, b3], axis=0), sp[...], NT)
     spatial = wide[:feats] + wide[feats : 2 * feats] + wide[2 * feats :]
     sq, sk, sv = (spatial[:, i * inner : (i + 1) * inner] for i in range(3))
     owner = lax.broadcasted_iota(jnp.int32, (feats, inner), 1) // HEAD_DIM
@@ -330,32 +355,32 @@
 
     sk3 = jnp.concatenate([sk] * 3 + [jnp.zeros((128 - 3 * feats, inner), F32)], axis=0)
     mixer = dot(by_head(sq), sk3, NT, HI) * (1.0 / math.sqrt(HEAD_DIM))
-    for h in range(HEADS):
-        mall[:, h * 128 : (h + 1) * 128] = mixer[h * feats : (h + 1) * feats]
-    v1, v2 = split2(by_head(sv))
-    weight_copies[1].wait()
+    mixer = jnp.concatenate(
+        [mixer[h * feats : (h + 1) * feats] for h in range(HEADS)], axis=1
+    )
+    mixer = jnp.concatenate(pieces(mixer, 3), axis=0)
+    v1, v2 = pieces(by_head(sv), 2)
+    weight_copies[2].wait()
     carried = dot(v1, so[...]) + dot(v2, so[...])
     carried = carried - jnp.mean(carried, axis=-1, keepdims=True)
-    rest = state.shape[0] - feats * (HEADS + 1)
-    full = jnp.concatenate([base_c, carried, jnp.zeros((rest, width), F32)], axis=0)
-    f1, f2 = split2(full)
-    full_hi[...] = f1
-    full_lo[...] = f2
-    gram[...] = (dot(f1, f1, NT) + dot(f1, f2, NT) + dot(f2, f1, NT)) * (1.0 / width)
-    weight_copies[2].wait()
-    g1, g2 = split2((dot(f1, tp[...]) + dot(f2, tp[...])).T)
-    gt_hi[...] = g1
-    gt_lo[...] = g2
+    rest = depth - feats * (HEADS + 2)
+    full[...] = jnp.concatenate(
+        [base_c, carried, base_c - b1.astype(F32), jnp.zeros((rest, width), F32)], axis=0
+    ).astype(jnp.bfloat16)
     small = dot(base_c, base_c, NT, HI) * (1.0 / width)
+    small = jnp.concatenate(pieces(small, 3), axis=0)
+    weight_copies[3].wait()
+    gt[...] = dot(tp[...], full[...], NT).astype(jnp.bfloat16)
 
     for k in range(1, peers):
-        x_copy(lax.rem(fi + k, peers)).wait_send()
+        other = lax.rem(fi + k, peers)
+        x_copy(other).wait_send()
         pltpu.make_async_remote_copy(
             src_ref=x_ref.at[pl.ds(0, window)],
-            dst_ref=near.at[lax.rem(fi + k, peers), pl.ds(0, window)],
-            send_sem=x_send.at[fi],
-            recv_sem=x_recv.at[lax.rem(fi + k, peers)],
-            device_id={"frame": lax.rem(fi + k, peers), "row": gi},
+            dst_ref=near.at[other, pl.ds(0, window)],
+            send_sem=x_send.at[other],
+            recv_sem=x_recv.at[other],
+            device_id={"frame": other, "row": gi},
             device_id_type=MESH,
         ).wait_recv()
     halos(lambda copy: copy.wait_send())
@@ -372,11 +397,10 @@
                 device_id_type=MESH,
             ).wait_recv()
 
-    mark = (
-        lax.broadcasted_iota(jnp.int32, (feats - ch, lanes), 1) // cols
-        == lax.broadcasted_iota(jnp.int32, (feats - ch, lanes), 0)
-    ).astype(F32)
-    spots, biases = [], []
+    span = -(-window * cols // lanes) * lanes
+    spots = []
+    key_lane = lax.broadcasted_iota(jnp.int32, (1, span), 1)
+    bias = jnp.full((1, span), -1e30, F32)
     for d in range(-REACH, REACH + 1):
         lr = fi + d
         spots.append(
@@ -387,57 +411,85 @@
             )
         )
         there = gi * rows_l + lr
-        biases.append(jnp.where((there >= 0) & (there < rows_l * halves), 0.0, -1e30).astype(F32))
-
+        level = jnp.where((there >= 0) & (there < rows_l * halves), 0.0, -1e30).astype(F32)
+        bias = jnp.where(key_lane // cols == d + REACH, level, bias)
+
+    tail = [jnp.zeros((ch, span - window * cols), F32)] if span > window * cols else []
+    groups, owns = [], []
+    for f in range(peers):
+        seen = [near[f, spot].astype(F32) for spot in spots]
+        owns.append(seen[REACH][:, :per])
+        for b in range(batches):
+            groups.append(
+                jnp.concatenate([v[:, b * cols : (b + 1) * cols] for v in seen] + tail, axis=1)
+            )
+
+    def lifted(value, video):
+        mark = (
+            video == lax.broadcasted_iota(jnp.int32, (feats - ch, value.shape[1]), 0)
+        ).astype(F32)
+        return jnp.concatenate([value, mark], axis=0)
+
+    def spread_of(value):
+        part = dot(small, value.astype(jnp.bfloat16))
+        part = part[:feats] + part[feats : 2 * feats] + part[2 * feats :]
+        var = jnp.sum(value * part, axis=0, keepdims=True)
+        return lax.rsqrt(jnp.maximum(var, 0.0) + 1e-06)
+
+    own = jnp.concatenate(owns, axis=1)
+    tokens = own.shape[1]
+    video = lax.broadcasted_iota(jnp.int32, (feats - ch, tokens), 1) % per // cols
+    own = lifted(own, video)
+    state[0:feats, :] = own
+    state[feats * (HEADS + 1) : feats * (HEADS + 2), :] = own
+    state[feats * (HEADS + 2) :, :] = jnp.zeros((rest, tokens), F32)
+    turned_own = jnp.concatenate(
+        [own] * 3 + [jnp.broadcast_to(spread_of(own), (128 - 3 * feats, tokens))], axis=0
+    ).T
+    ask = dot(turned_own[:, : 3 * feats].astype(jnp.bfloat16), mixer)
+    ask = ask * turned_own[:, 3 * feats : 3 * feats + 1]
+    lead = ask.astype(jnp.bfloat16).astype(F32)
+    lane = lax.broadcasted_iota(jnp.int32, ask.shape, 1) % 128
+    ask3 = jnp.where(lane < 2 * feats, lead, ask - lead).astype(jnp.bfloat16)
+
+    key_video = [
+        jnp.full((feats - ch, span), b, jnp.int32) for b in range(batches)
+    ]
     tiles_of_u = []
-    for f in range(peers):
-        lifted = jnp.concatenate(
+    for g, value in enumerate(groups):
+        value = lifted(value, key_video[g % batches])
+        y = value * spread_of(value)
+        high = y.astype(jnp.bfloat16)
+        low = y - high.astype(F32)
+        high = high.astype(F32)
+        keys3 = jnp.concatenate(
+            [high, low, high, jnp.zeros((128 - 3 * feats, span), F32)], axis=0
+        ).astype(jnp.bfloat16)
+        values = jnp.concatenate([high, low, jnp.ones((16, span), F32)], axis=0)
+        q3 = jnp.concatenate(
             [
-                jnp.concatenate([near[f, spot].astype(F32), mark], axis=0)
-                for spot in spots
+                ask3[g * cols : (g + 1) * cols, h * 128 : (h + 1) * 128]
+                for h in range(HEADS)
             ],
-            axis=1,
-        )
-        var = jnp.sum(lifted * dot(small, lifted, precision=HI), axis=0, keepdims=True)
-        y = lifted * lax.rsqrt(jnp.maximum(var, 0.0) + 1e-06)
-        high = y.astype(jnp.bfloat16).astype(F32)
-        keys3 = jnp.concatenate(
-            [high, y - high, high, jnp.zeros((128 - 3 * feats, window * lanes), F32)], axis=0
-        )
-        keys3 = [keys3[:, i * lanes : (i + 1) * lanes].T for i in range(window)]
-        own = y[:, REACH * lanes : (REACH + 1) * lanes].T[:per]
-        ask = dot(own, mall[...], precision=HI)
-        lead = ask.astype(jnp.bfloat16).astype(F32)
-        lane = lax.broadcasted_iota(jnp.int32, ask.shape, 1) % 128
-        ask3 = jnp.where(lane < 2 * feats, lead, ask - lead).astype(jnp.bfloat16)
-        state[0:feats, f * per : (f + 1) * per] = lifted[
-            :, REACH * lanes : REACH * lanes + per
-        ]
-        for b in range(batches):
-            cut = slice(b * cols, (b + 1) * cols)
-            k3 = jnp.concatenate([k[cut] for k in keys3], axis=0).astype(jnp.bfloat16)
-            q3 = jnp.concatenate(
-                [ask3[cut, h * 128 : (h + 1) * 128] for h in range(HEADS)], axis=0
-            )
-            scores = dot(k3, q3, NT)
-            scores = jnp.concatenate(
-                [scores[i * cols : (i + 1) * cols] + biases[i] for i in range(window)], axis=0
-            )
-            weight = jnp.exp(scores - jnp.max(scores, axis=0, keepdims=True))
-            weight = weight * (1.0 / jnp.sum(weight, axis=0, keepdims=True))
-            both = dot(k3, weight.astype(jnp.bfloat16), ((0,), (0,)))
-            tiles_of_u.append(both[:feats] + both[feats : 2 * feats])
+            axis=0,
+        )
+        scores = dot(q3, keys3) + bias
+        weight = jnp.exp(scores - jnp.max(scores, axis=1, keepdims=True))
+        both = dot(values.astype(jnp.bfloat16), weight.astype(jnp.bfloat16), NT)
+        tiles_of_u.append(
+            (both[:feats] + both[feats : 2 * feats]) * (1.0 / both[2 * feats : 2 * feats + 1])
+        )
     for h in range(HEADS):
         state[feats * (h + 1) : feats * (h + 2), :] = jnp.concatenate(
             [u[:, h * cols : (h + 1) * cols] for u in tiles_of_u], axis=1
         )
-    state[feats * (HEADS + 1) :, :] = jnp.zeros((rest, state.shape[1]), F32)
 
     z = state[...]
-    z1, z2 = split2(z)
-    var = jnp.sum(z * (dot(gram[...], z, precision=HI)), axis=0, keepdims=True)
-    share = lax.rsqrt(jnp.maximum(var, 0.0) + 1e-06)
-    qkv[...] = (dot(gt_hi[...], z1) + dot(gt_hi[...], z2) + dot(gt_lo[...], z1)) * share
+    stream1[...] = dot(z.T.astype(jnp.bfloat16), full[...])
+    square = stream1[...]
+    square = (square * square).astype(jnp.bfloat16)
+    var = dot(jnp.ones((16, width), jnp.bfloat16), square, NT)[0:1] * (1.0 / width)
+    qkv[...] = dot(gt[...], z.astype(jnp.bfloat16)) * lax.rsqrt(var + 1e-06)
     tiles = peers // pair
     scale = 1.0 / math.sqrt(HEAD_DIM)
 
@@ -462,23 +514,21 @@
             )
             mixed_t[h * HEAD_DIM : (h + 1) * HEAD_DIM, p * lanes : (p + 1) * lanes] = acc
 
-    zt = z.T
-    zt1, zt2 = split2(zt)
-    weight_copies[3].wait()
-    stream = dot(zt1, full_hi[...]) + dot(zt2, full_hi[...]) + dot(zt1, full_lo[...])
-    stream = stream + dot(mixed_t[...].T.astype(jnp.bfloat16), to[...])
+    weight_copies[4].wait()
+    stream = stream1[...] + dot(mixed_t[...].T.astype(jnp.bfloat16), to[...])
     stream = stream - jnp.mean(stream, axis=-1, keepdims=True)
     share = lax.rsqrt(jnp.mean(stream * stream, axis=-1, keepdims=True) + 1e-06)
     predicted = dot(final_ref[...], (stream * share).astype(jnp.bfloat16), NT)
 
     for k in range(1, peers):
-        t_copy(lax.rem(fi + k, peers)).wait_send()
+        other = lax.rem(fi + k, peers)
+        t_copy(other).wait_send()
         pltpu.make_async_remote_copy(
             src_ref=target_ref.at[0],
-            dst_ref=goal.at[lax.rem(fi + k, peers)],
-            send_sem=t_send.at[fi],
-            recv_sem=t_recv.at[lax.rem(fi + k, peers)],
-            device_id={"frame": lax.rem(fi + k, peers), "row": gi},
+            dst_ref=goal.at[other],
+            send_sem=t_send.at[other],
+            recv_sem=t_recv.at[other],
+            device_id={"frame": other, "row": gi},
             device_id_type=MESH,
         ).wait_recv()
     aim = jnp.concatenate([goal[f][:, :per] for f in range(peers)], axis=1)
@@ -498,7 +548,8 @@
         )
 
     for k in range(1, peers):
-        e_copy(lax.rem(fi + k, peers), fi, lax.rem(fi + k, peers)).start()
+        other = lax.rem(fi + k, peers)
+        e_copy(other, fi, other).start()
     err_in[fi] = err_out[fi // pair]
     for k in range(1, peers):
         other = lax.rem(fi + k, peers)
@@ -508,7 +559,8 @@
     result = got[:, :per]
     for s in range(1, pair):
         result = jnp.where(lax.rem(fi, pair) == s, got[:, s * per : (s + 1) * per], result)
-    out_ref[...] = result
+    for b in range(batches):
+        out_ref[b, 0] = result[:, b * cols : (b + 1) * cols]
 
 
 def fused(
@@ -523,57 +575,39 @@
     temporal_output,
     final_weight,
 ):
-    batches, _, rows_l, cols, ch = latents.shape
+    batches, frames_l, rows_l, cols, ch = latents.shape
     peers, halves = lax.axis_size("frame"), lax.axis_size("row")
     width, inner = patch_weight.shape[1], spatial_output.shape[0]
     per, lanes = batches * cols, 128
-    signal, spread = noise_levels(timesteps)
-    noisy = (
-        signal[:, None, None, None, None] * latents
-        + spread[:, None, None, None, None] * target_noise
-    ).astype(jnp.bfloat16)
-
-    def channel_major(value):
-        value = value[:, 0].transpose(1, 3, 0, 2).reshape(rows_l, ch, per)
-        return jnp.pad(value, ((0, 0), (0, 0), (0, lanes - per)))
-
-    feats = -(-(ch + batches) // 8) * 8
-    time_vector = time_embed(timesteps, time_weight)
-    base = jnp.concatenate(
-        [
-            patch_weight.astype(F32),
-            time_vector,
-            jnp.zeros((feats - ch - batches, width), F32),
-        ],
-        axis=0,
-    )
+    feats = ch + 8
     tokens = peers * per
-    depth = -(-(feats * (HEADS + 1)) // 128) * 128
+    depth = -(-(feats * (HEADS + 2)) // 128) * 128
     bf16 = jnp.bfloat16
     vmem, anywhere = pl.BlockSpec(memory_space=pltpu.VMEM), pl.BlockSpec(memory_space=pl.ANY)
+    smem = pl.BlockSpec(memory_space=pltpu.SMEM)
     sems = pltpu.SemaphoreType.DMA
-    out = pl.pallas_call(
-        functools.partial(fused_kernel, peers, halves, batches, cols),
-        out_shape=jax.ShapeDtypeStruct((rows_l, per), F32),
-        in_specs=[vmem] * 4 + [anywhere] * 4,
+    return pl.pallas_call(
+        functools.partial(fused_kernel, peers, halves),
+        out_shape=jax.ShapeDtypeStruct((batches, frames_l, rows_l, cols), F32),
+        in_specs=[smem] + [vmem] * 4 + [anywhere] * 5,
         out_specs=vmem,
         scratch_shapes=[
-            pltpu.VMEM(spatial_project.shape, bf16),
+            pltpu.VMEM(time_weight.shape, bf16),
+            pltpu.VMEM(spatial_project.shape[::-1], bf16),
             pltpu.VMEM(spatial_output.shape, bf16),
-            pltpu.VMEM(temporal_project.shape, bf16),
+            pltpu.VMEM(temporal_project.shape[::-1], bf16),
             pltpu.VMEM(temporal_output.shape, bf16),
-            sems((4,)),
+            sems((5,)),
+            pltpu.VMEM((rows_l, ch, lanes), bf16),
+            pltpu.VMEM((rows_l, ch, lanes), F32),
             pltpu.VMEM((peers, 3 * REACH + 1, ch, lanes), bf16),
             pltpu.VMEM((peers, ch, lanes), F32),
             pltpu.VMEM((tokens // lanes, 8, lanes), F32),
             pltpu.VMEM((peers, 8, lanes), F32),
-            pltpu.VMEM((feats, HEADS * 128), F32),
             pltpu.VMEM((depth, width), bf16),
-            pltpu.VMEM((depth, width), bf16),
-            pltpu.VMEM((depth, depth), F32),
-            pltpu.VMEM((3 * inner, depth), bf16),
             pltpu.VMEM((3 * inner, depth), bf16),
             pltpu.VMEM((depth, tokens), F32),
+            pltpu.VMEM((tokens, width), F32),
             pltpu.VMEM((3 * inner, tokens), F32),
             pltpu.VMEM((inner, tokens), F32),
             sems((peers,)),
@@ -592,16 +626,17 @@
             flops=4 * 10**9, bytes_accessed=11 * 10**6, transcendentals=10**6
         ),
     )(
-        channel_major(noisy),
-        channel_major(target_noise),
-        base,
+        timesteps,
+        latents.transpose(0, 1, 2, 4, 3),
+        target_noise.transpose(0, 1, 2, 4, 3),
+        patch_weight,
         final_weight.T,
-        spatial_project,
+        time_weight,
+        spatial_project.T,
         spatial_output,
-        temporal_project,
+        temporal_project.T,
         temporal_output,
     )
-    return out.reshape(rows_l, batches, cols).transpose(1, 0, 2)[:, None]
 
 
 def fits(latents):
@@ -614,7 +649,8 @@
         and 128 % per == 0
         and (rows_l * per) % 128 == 0
         and ch % 16 == 0
-        and 3 * (ch + batches) <= 96
+        and batches <= 8
+        and 3 * (ch + 8) < 128
     )
 
 

time: 56.9 us -> 34.8 us (0.61)
  local copies, waits for them, and re-layouts: 17.1 us -> 1.3 us
  other arithmetic: 3.81 us -> 0 us
  matrix products: 1.07 us -> 0 us
  Pallas kernels: 34.3 us -> 33.3 us
    unnamed x4 -> x1, local copies, waits for them, and re-layouts: 12.9 us -> 1.3 us
    reshape x5 -> x0, local copies, waits for them, and re-layouts: 1.59 us -> none  [the longest x2 1.36 us: fused(): return out.reshape(rows_l, batches, cols).transpose(1, 0, 2)[:, None]]
    convert_element_type x2 -> x0, other arithmetic: 1.49 us -> none  [the longest x1 0.77 us: fused(): patch_weight.astype(F32)]
    pad x2 -> x0, local copies, waits for them, and re-layouts: 1.25 us -> none  [channel_major(): return jnp.pad(value, ((0, 0), (0, 0), (0, lanes - per)))]
    transpose x2 -> x0, local copies, waits for them, and re-layouts: 1.08 us -> none  [channel_major(): value = value[:, 0].transpose(1, 3, 0, 2).reshape(rows_l, ch, per)]
    transpose x1 -> x0, other arithmetic: 1.07 us -> none  [channel_major(): value = value[:, 0].transpose(1, 3, 0, 2).reshape(rows_l, ch, per)]
    dot_general x2 -> x0, matrix products: 1.07 us -> none  [the longest x1 0.88 us: noise_levels(): log_bar = jnp.dot(selector, log_keep, precision=HI)]
    pallas_call x1, Pallas kernels: 34.3 us -> 33.3 us  [fused(): pl.pallas_call(functools.partial(fused_kernel, peers, halves), out_shape=...]
where the time goes in v1:
time: 34.8 us; the launch traced here: 34.6 us
  Pallas kernels  33.3 us (96%)
  local copies, waits for them, and re-layouts  1.3 us (4%)
    pallas_call x1, Pallas kernels, fused(): pl.pallas_call(functools.partial(fused_kernel, peers, halves), out_shape=...  33.3 us
    unnamed x1, local copies, waits for them, and re-layouts  1.3 us

profile of v1, /device:TPU:0, one launch (start us, length us, event | category | flops | bytes accessed | tf_op | source)
XLA Modules:
  0.0 34.6 jit_solution(10425831829989637815)
XLA Ops:
  0.0 33.3 %shard_map.100 = f32[2,1,8,32]{3,2,1,0:T(8,128)} custom-call(s32[2]{0:T(128)} %times_ref.1, f32[2,1,8,16,32]{4,3,2,1,0:T(8,128)} %bitcast.7, f32[2,1,8,16,32]{4,3,2,1,0:T(8,128)} %bitcast.8, bf16[16,1152]{1,0:T(8,128)(2,1)} %patch_ref.1, bf16[16,1152]{1,0:T(8,128)(2,1)} %bitcast.9, bf16[256,1152]{1,0:T(8,128)(2,1)} %tw_hbm.1, bf16[1728,1152]{1,0:T(8,128)(2,1)} %bitcast.5, ...), custom_call_target="tpu_custom_call" | custom-call | flops 4000000000 | bytes 11000000 | tf_op jit(solution)/shard_map/pallas_call | solution.py:589
  33.3 1.3 %copy.12 = f32[2,1,8,32]{3,2,1,0:T(8,128)} copy(f32[2,1,8,32]{3,2,1,0:T(8,128)} %shard_map.100) | data formatting | bytes 4096

commit v2 on v1

--- a/solution.py
+++ b/solution.py
@@ -12,6 +12,7 @@
 HEADS = 8
 STEPS = 1000
 REACH = 2
+STAGE = 8
 HI = lax.Precision.HIGHEST
 F32 = jnp.float32
 MESH = pl.DeviceIdType.MESH
@@ -450,35 +451,47 @@
     ask = ask * turned_own[:, 3 * feats : 3 * feats + 1]
     lead = ask.astype(jnp.bfloat16).astype(F32)
     lane = lax.broadcasted_iota(jnp.int32, ask.shape, 1) % 128
-    ask3 = jnp.where(lane < 2 * feats, lead, ask - lead).astype(jnp.bfloat16)
-
-    key_video = [
-        jnp.full((feats - ch, span), b, jnp.int32) for b in range(batches)
-    ]
+    ask3 = jnp.where(lane < 2 * feats, lead, ask - lead)
+    ask3 = jnp.where(lane == 3 * feats, 1.0, ask3).astype(jnp.bfloat16)
+
+    count = len(groups)
+    near_all = jnp.concatenate(groups, axis=1)
+    video = lax.broadcasted_iota(jnp.int32, (feats - ch, count * span), 1) // span % batches
+    near_all = lifted(near_all, video)
+    y = near_all * spread_of(near_all)
+    high = y.astype(jnp.bfloat16).astype(F32)
+    low = y - high
+    blocked = jnp.concatenate([bias] * count, axis=1)
+    keys3 = jnp.concatenate(
+        [high, low, high, blocked, jnp.zeros((127 - 3 * feats, count * span), F32)], axis=0
+    ).astype(jnp.bfloat16)
+    values = jnp.concatenate([high, low, jnp.ones((16, count * span), F32)], axis=0)
+    values = values.astype(jnp.bfloat16)
     tiles_of_u = []
-    for g, value in enumerate(groups):
-        value = lifted(value, key_video[g % batches])
-        y = value * spread_of(value)
-        high = y.astype(jnp.bfloat16)
-        low = y - high.astype(F32)
-        high = high.astype(F32)
-        keys3 = jnp.concatenate(
-            [high, low, high, jnp.zeros((128 - 3 * feats, span), F32)], axis=0
-        ).astype(jnp.bfloat16)
-        values = jnp.concatenate([high, low, jnp.ones((16, span), F32)], axis=0)
-        q3 = jnp.concatenate(
-            [
-                ask3[g * cols : (g + 1) * cols, h * 128 : (h + 1) * 128]
-                for h in range(HEADS)
-            ],
-            axis=0,
-        )
-        scores = dot(q3, keys3) + bias
-        weight = jnp.exp(scores - jnp.max(scores, axis=1, keepdims=True))
-        both = dot(values.astype(jnp.bfloat16), weight.astype(jnp.bfloat16), NT)
-        tiles_of_u.append(
-            (both[:feats] + both[feats : 2 * feats]) * (1.0 / both[2 * feats : 2 * feats + 1])
-        )
+    for first in range(0, count, STAGE):
+        some = range(first, min(first + STAGE, count))
+        scores = [
+            dot(
+                jnp.concatenate(
+                    [
+                        ask3[g * cols : (g + 1) * cols, h * 128 : (h + 1) * 128]
+                        for h in range(HEADS)
+                    ],
+                    axis=0,
+                ),
+                keys3[:, g * span : (g + 1) * span],
+            )
+            for g in some
+        ]
+        tops = [jnp.max(v, axis=1, keepdims=True) for v in scores]
+        weights = [jnp.exp(v - t).astype(jnp.bfloat16) for v, t in zip(scores, tops)]
+        sums = [
+            dot(values[:, g * span : (g + 1) * span], w, NT) for g, w in zip(some, weights)
+        ]
+        tiles_of_u += [
+            (v[:feats] + v[feats : 2 * feats]) * (1.0 / v[2 * feats : 2 * feats + 1])
+            for v in sums
+        ]
     for h in range(HEADS):
         state[feats * (h + 1) : feats * (h + 2), :] = jnp.concatenate(
             [u[:, h * cols : (h + 1) * cols] for u in tiles_of_u], axis=1
@@ -500,19 +513,27 @@
     def turned(value, s):
         return pltpu.roll(value, s * per, 1) if s else value
 
+    shifts = [(t, s) for t in range(tiles) for s in range(pair)]
+    logits = [[[] for _ in shifts] for _ in range(tiles)]
     for h in range(HEADS):
-        ks = [turned(tile_of(1, h, t), s) for t in range(tiles) for s in range(pair)]
-        vs = [turned(tile_of(2, h, t), s) for t in range(tiles) for s in range(pair)]
+        ks = [turned(tile_of(1, h, t), s) for t, s in shifts]
         for p in range(tiles):
             q = tile_of(0, h, p) * scale
-            logits = [jnp.sum(q * k, axis=0, keepdims=True) for k in ks]
-            top = functools.reduce(jnp.maximum, logits)
-            exps = [jnp.exp(s - top) for s in logits]
-            total = 1.0 / functools.reduce(jnp.add, exps)
-            acc = functools.reduce(
-                jnp.add, [(e * total) * v for e, v in zip(exps, vs)]
+            for slot, k in zip(logits[p], ks):
+                slot.append(jnp.sum(q * k, axis=0, keepdims=True))
+    shares = []
+    for p in range(tiles):
+        rows = [jnp.concatenate(slot, axis=0) for slot in logits[p]]
+        top = functools.reduce(jnp.maximum, rows)
+        exps = [jnp.exp(v - top) for v in rows]
+        total = 1.0 / functools.reduce(jnp.add, exps)
+        shares.append([e * total for e in exps])
+    for h in range(HEADS):
+        vs = [turned(tile_of(2, h, t), s) for t, s in shifts]
+        for p in range(tiles):
+            mixed_t[h * HEAD_DIM : (h + 1) * HEAD_DIM, p * lanes : (p + 1) * lanes] = (
+                functools.reduce(jnp.add, [w[h : h + 1] * v for w, v in zip(shares[p], vs)])
             )
-            mixed_t[h * HEAD_DIM : (h + 1) * HEAD_DIM, p * lanes : (p + 1) * lanes] = acc
 
     weight_copies[4].wait()
     stream = stream1[...] + dot(mixed_t[...].T.astype(jnp.bfloat16), to[...])
@@ -533,7 +554,7 @@
         ).wait_recv()
     aim = jnp.concatenate([goal[f][:, :per] for f in range(peers)], axis=1)
     gap = predicted - aim
-    errors = jnp.mean(gap * gap, axis=0, keepdims=True)
+    errors = jnp.sum(gap * gap, axis=0, keepdims=True)
     for t in range(tiles):
         err_out[t] = jnp.broadcast_to(errors[:, t * lanes : (t + 1) * lanes], (8, lanes))
 
@@ -586,7 +607,7 @@
     vmem, anywhere = pl.BlockSpec(memory_space=pltpu.VMEM), pl.BlockSpec(memory_space=pl.ANY)
     smem = pl.BlockSpec(memory_space=pltpu.SMEM)
     sems = pltpu.SemaphoreType.DMA
-    return pl.pallas_call(
+    summed = pl.pallas_call(
         functools.partial(fused_kernel, peers, halves),
         out_shape=jax.ShapeDtypeStruct((batches, frames_l, rows_l, cols), F32),
         in_specs=[smem] + [vmem] * 4 + [anywhere] * 5,
@@ -637,6 +658,7 @@
         temporal_project.T,
         temporal_output,
     )
+    return summed * (1.0 / ch)
 
 
 def fits(latents):

time: 34.8 us -> 29.4 us (0.84)
  Pallas kernels: 33.3 us -> 27.9 us
  other arithmetic: 0 us -> 1.3 us
  local copies, waits for them, and re-layouts: 1.3 us -> 0 us
    pallas_call x1, Pallas kernels: 33.3 us -> 27.9 us  [fused(): pl.pallas_call(functools.partial(fused_kernel, peers, halves), out_shape=...]
    mul x0 -> x1, other arithmetic: none -> 1.3 us  [fused(): return summed * (1.0 / ch)]
    unnamed x1 -> x0, local copies, waits for them, and re-layouts: 1.3 us -> none
where the time goes in v2:
time: 29.4 us; the launch traced here: 29.2 us
  Pallas kernels  27.9 us (95%)
  other arithmetic  1.3 us (4%)
    pallas_call x1, Pallas kernels, fused(): pl.pallas_call(functools.partial(fused_kernel, peers, halves), out_shape=...  27.9 us
    mul x1, other arithmetic, fused(): return summed * (1.0 / ch)  1.3 us

profile of v2, /device:TPU:0, one launch (start us, length us, event | category | flops | bytes accessed | tf_op | source)
XLA Modules:
  0.0 29.2 jit_solution(7969406431320848944)
XLA Ops:
  0.0 27.9 %shard_map.100 = f32[2,1,8,32]{3,2,1,0:T(8,128)} custom-call(s32[2]{0:T(128)} %times_ref.1, f32[2,1,8,16,32]{4,3,2,1,0:T(8,128)} %bitcast.7, f32[2,1,8,16,32]{4,3,2,1,0:T(8,128)} %bitcast.8, bf16[16,1152]{1,0:T(8,128)(2,1)} %patch_ref.1, bf16[16,1152]{1,0:T(8,128)(2,1)} %bitcast.9, bf16[256,1152]{1,0:T(8,128)(2,1)} %tw_hbm.1, bf16[1728,1152]{1,0:T(8,128)(2,1)} %bitcast.5, ...), custom_call_target="tpu_custom_call" | custom-call | flops 4000000000 | bytes 11000000 | tf_op jit(solution)/shard_map/pallas_call | solution.py:610
  27.9 1.3 %broadcast_multiply_fusion = f32[2,1,8,32]{3,2,1,0:T(8,128)} fusion(f32[2,1,8,32]{3,2,1,0:T(8,128)} %shard_map.100), kind=kLoop, calls=%fused_computation | loop fusion | flops 512 | bytes 4096 | tf_op jit(solution)/shard_map/mul | solution.py:661

commit v3 on v2

--- a/solution.py
+++ b/solution.py
@@ -12,7 +12,7 @@
 HEADS = 8
 STEPS = 1000
 REACH = 2
-STAGE = 8
+STAGE = 16
 HI = lax.Precision.HIGHEST
 F32 = jnp.float32
 MESH = pl.DeviceIdType.MESH
@@ -230,13 +230,14 @@
     inner = so.shape[0]
     feats = ch + 8
     depth = full.shape[0]
+    rest = depth - feats * (HEADS + 2)
     window = 2 * REACH + 1
     fi, gi = lax.axis_index("frame"), lax.axis_index("row")
     pairs = ((tw_hbm, tw), (sp_hbm, sp), (so_hbm, so), (tp_hbm, tp), (to_hbm, to))
     weight_copies = [
         pltpu.make_async_copy(src, dst, w_sem.at[i]) for i, (src, dst) in enumerate(pairs)
     ]
-    for copy in weight_copies:
+    for copy in weight_copies[:2]:
         copy.start()
 
     barrier = pltpu.get_barrier_semaphore()
@@ -344,6 +345,8 @@
     base_c = base - jnp.mean(base, axis=-1, keepdims=True)
     b1, b2, b3 = pieces(base_c, 3)
     weight_copies[1].wait()
+    for copy in weight_copies[2:]:
+        copy.start()
     wide = dot(jnp.concatenate([b1, b2, b3], axis=0), sp[...], NT)
     spatial = wide[:feats] + wide[feats : 2 * feats] + wide[2 * feats :]
     sq, sk, sv = (spatial[:, i * inner : (i + 1) * inner] for i in range(3))
@@ -360,18 +363,8 @@
         [mixer[h * feats : (h + 1) * feats] for h in range(HEADS)], axis=1
     )
     mixer = jnp.concatenate(pieces(mixer, 3), axis=0)
-    v1, v2 = pieces(by_head(sv), 2)
-    weight_copies[2].wait()
-    carried = dot(v1, so[...]) + dot(v2, so[...])
-    carried = carried - jnp.mean(carried, axis=-1, keepdims=True)
-    rest = depth - feats * (HEADS + 2)
-    full[...] = jnp.concatenate(
-        [base_c, carried, base_c - b1.astype(F32), jnp.zeros((rest, width), F32)], axis=0
-    ).astype(jnp.bfloat16)
     small = dot(base_c, base_c, NT, HI) * (1.0 / width)
     small = jnp.concatenate(pieces(small, 3), axis=0)
-    weight_copies[3].wait()
-    gt[...] = dot(tp[...], full[...], NT).astype(jnp.bfloat16)
 
     for k in range(1, peers):
         other = lax.rem(fi + k, peers)
@@ -397,6 +390,10 @@
                 device_id={"frame": k, "row": lax.rem(gi + 1, halves)},
                 device_id_type=MESH,
             ).wait_recv()
+
+    weight_copies[2].wait()
+    weight_copies[3].wait()
+    weight_copies[4].wait()
 
     span = -(-window * cols // lanes) * lanes
     spots = []
@@ -454,6 +451,13 @@
     ask3 = jnp.where(lane < 2 * feats, lead, ask - lead)
     ask3 = jnp.where(lane == 3 * feats, 1.0, ask3).astype(jnp.bfloat16)
 
+    v1, v2 = pieces(by_head(sv), 2)
+    carried = dot(v1, so[...]) + dot(v2, so[...])
+    carried = carried - jnp.mean(carried, axis=-1, keepdims=True)
+    full[...] = jnp.concatenate(
+        [base_c, carried, base_c - b1.astype(F32), jnp.zeros((rest, width), F32)], axis=0
+    ).astype(jnp.bfloat16)
+    gt[...] = dot(tp[...], full[...], NT).astype(jnp.bfloat16)
     count = len(groups)
     near_all = jnp.concatenate(groups, axis=1)
     video = lax.broadcasted_iota(jnp.int32, (feats - ch, count * span), 1) // span % batches
@@ -535,7 +539,6 @@
                 functools.reduce(jnp.add, [w[h : h + 1] * v for w, v in zip(shares[p], vs)])
             )
 
-    weight_copies[4].wait()
     stream = stream1[...] + dot(mixed_t[...].T.astype(jnp.bfloat16), to[...])
     stream = stream - jnp.mean(stream, axis=-1, keepdims=True)
     share = lax.rsqrt(jnp.mean(stream * stream, axis=-1, keepdims=True) + 1e-06)

time: 29.4 us -> 30.6 us (1.041)
  Pallas kernels: 27.9 us -> 29.1 us
    pallas_call x1, Pallas kernels: 27.9 us -> 29.1 us  [fused(): pl.pallas_call(functools.partial(fused_kernel, peers, halves), out_shape=...]
where the time goes in v3:
time: 30.6 us; the launch traced here: 30.4 us
  Pallas kernels  29.1 us (95%)
  other arithmetic  1.3 us (4%)
    pallas_call x1, Pallas kernels, fused(): pl.pallas_call(functools.partial(fused_kernel, peers, halves), out_shape=...  29.1 us
    mul x1, other arithmetic, fused(): return summed * (1.0 / ch)  1.3 us

profile of v3, /device:TPU:0, one launch (start us, length us, event | category | flops | bytes accessed | tf_op | source)
XLA Modules:
  0.0 30.4 jit_solution(10083497787054221133)
XLA Ops:
  0.0 29.1 %shard_map.100 = f32[2,1,8,32]{3,2,1,0:T(8,128)} custom-call(s32[2]{0:T(128)} %times_ref.1, f32[2,1,8,16,32]{4,3,2,1,0:T(8,128)} %bitcast.7, f32[2,1,8,16,32]{4,3,2,1,0:T(8,128)} %bitcast.8, bf16[16,1152]{1,0:T(8,128)(2,1)} %patch_ref.1, bf16[16,1152]{1,0:T(8,128)(2,1)} %bitcast.9, bf16[256,1152]{1,0:T(8,128)(2,1)} %tw_hbm.1, bf16[1728,1152]{1,0:T(8,128)(2,1)} %bitcast.5, ...), custom_call_target="tpu_custom_call" | custom-call | flops 4000000000 | bytes 11000000 | tf_op jit(solution)/shard_map/pallas_call | solution.py:613
  29.1 1.3 %broadcast_multiply_fusion = f32[2,1,8,32]{3,2,1,0:T(8,128)} fusion(f32[2,1,8,32]{3,2,1,0:T(8,128)} %shard_map.100), kind=kLoop, calls=%fused_computation | loop fusion | flops 512 | bytes 4096 | tf_op jit(solution)/shard_map/mul | solution.py:664

commit v4 on v2

--- a/solution.py
+++ b/solution.py
@@ -265,7 +265,18 @@
         signal, spread = jnp.sqrt(kept)[None], jnp.sqrt(1.0 - kept)[None]
         noisy.append(signal * lat_ref[b, 0] + spread * noise_ref[b, 0])
     blank = [jnp.zeros((rows_l, ch, lanes - per), F32)] if lanes > per else []
-    x_ref[...] = jnp.concatenate(noisy + blank, axis=2).astype(jnp.bfloat16)
+    rows = jnp.concatenate(noisy, axis=2)
+    packed = window // 2 + 1
+    empty = jnp.zeros((1, ch, per), F32)
+    ahead = jnp.concatenate([rows[packed:], empty], axis=0)
+    x_ref[0 : rows_l - packed + 1] = jnp.concatenate(
+        [rows[: rows_l - packed + 1], ahead], axis=2
+    ).astype(jnp.bfloat16)
+    edges = ((rows_l - REACH, rows_l - REACH + 1), (0, 1))
+    for i, (one, two) in enumerate(edges):
+        x_ref[rows_l - packed + 1 + i] = jnp.concatenate(
+            [rows[one], rows[two]], axis=1
+        ).astype(jnp.bfloat16)
     target_ref[...] = jnp.concatenate(
         [noise_ref[b, 0] for b in range(batches)] + blank, axis=2
     )
@@ -276,8 +287,8 @@
 
     def x_copy(peer):
         return pltpu.make_async_remote_copy(
-            src_ref=x_ref.at[pl.ds(start_of(peer), window)],
-            dst_ref=near.at[fi, pl.ds(0, window)],
+            src_ref=x_ref.at[pl.ds(start_of(peer), packed)],
+            dst_ref=near.at[fi, pl.ds(0, packed)],
             send_sem=x_send.at[peer],
             recv_sem=x_recv.at[fi],
             device_id={"frame": peer, "row": gi},
@@ -296,8 +307,8 @@
 
     def halo_copy(slot, peer, half, first):
         return pltpu.make_async_remote_copy(
-            src_ref=x_ref.at[pl.ds(first, REACH)],
-            dst_ref=near.at[fi, pl.ds(window, REACH)],
+            src_ref=x_ref.at[first],
+            dst_ref=near.at[fi, packed],
             send_sem=h_send.at[slot],
             recv_sem=h_recv.at[fi],
             device_id={"frame": peer, "row": half},
@@ -309,24 +320,24 @@
 
             @pl.when(gi < halves - 1)
             def _():
-                action(halo_copy(i, i, gi + 1, rows_l - REACH))
+                action(halo_copy(i, i, gi + 1, rows_l - packed + 1))
 
             @pl.when(gi > 0)
             def _():
-                action(halo_copy(REACH + i, peers - REACH + i, gi - 1, 0))
+                action(halo_copy(REACH + i, peers - REACH + i, gi - 1, rows_l - packed + 2))
 
     for k in range(1, peers):
         x_copy(lax.rem(fi + k, peers)).start()
     halos(lambda copy: copy.start())
     for k in range(1, peers):
         t_copy(lax.rem(fi + k, peers)).start()
-    near[fi, 0:window] = x_ref[pl.ds(start_of(fi), window)]
+    near[fi, 0:packed] = x_ref[pl.ds(start_of(fi), packed)]
     goal[fi] = target_ref[fi]
     takes_halo = ((fi < REACH) & (gi > 0)) | ((fi >= peers - REACH) & (gi < halves - 1))
 
     @pl.when(jnp.logical_not(takes_halo))
     def _():
-        near[:, window:] = jnp.zeros((peers, REACH, ch, lanes), near.dtype)
+        near[:, packed:] = jnp.zeros((peers, 1, ch, lanes), near.dtype)
 
     halfway = tw.shape[0] // 2
     row = lax.broadcasted_iota(jnp.int32, (8, halfway), 0)
@@ -371,14 +382,17 @@
     small = dot(base_c, base_c, NT, HI) * (1.0 / width)
     small = jnp.concatenate(pieces(small, 3), axis=0)
     weight_copies[3].wait()
-    gt[...] = dot(tp[...], full[...], NT).astype(jnp.bfloat16)
+    turned_full = dot(tp[...], full[...], NT)
+    scale = 1.0 / math.sqrt(HEAD_DIM)
+    gt[0:inner] = (turned_full[:inner] * scale).astype(jnp.bfloat16)
+    gt[inner:] = turned_full[inner:].astype(jnp.bfloat16)
 
     for k in range(1, peers):
         other = lax.rem(fi + k, peers)
         x_copy(other).wait_send()
         pltpu.make_async_remote_copy(
-            src_ref=x_ref.at[pl.ds(0, window)],
-            dst_ref=near.at[other, pl.ds(0, window)],
+            src_ref=x_ref.at[pl.ds(0, packed)],
+            dst_ref=near.at[other, pl.ds(0, packed)],
             send_sem=x_send.at[other],
             recv_sem=x_recv.at[other],
             device_id={"frame": other, "row": gi},
@@ -390,8 +404,8 @@
     def _():
         for k in range(peers):
             pltpu.make_async_remote_copy(
-                src_ref=x_ref.at[pl.ds(0, REACH)],
-                dst_ref=near.at[k, pl.ds(window, REACH)],
+                src_ref=x_ref.at[0],
+                dst_ref=near.at[k, packed],
                 send_sem=h_send.at[0],
                 recv_sem=h_recv.at[k],
                 device_id={"frame": k, "row": lax.rem(gi + 1, halves)},
@@ -404,13 +418,11 @@
     bias = jnp.full((1, span), -1e30, F32)
     for d in range(-REACH, REACH + 1):
         lr = fi + d
-        spots.append(
-            jnp.where(
-                lr < 0,
-                window + lr + REACH,
-                jnp.where(lr >= rows_l, window + lr - rows_l, lr - start_of(fi)),
-            )
-        )
+        outside = (lr < 0) | (lr >= rows_l)
+        step = jnp.where(lr < 0, lr + REACH, jnp.where(lr >= rows_l, lr - rows_l, lr - start_of(fi)))
+        second = jnp.where(outside, step == 1, step >= packed)
+        entry = jnp.where(outside, packed, jnp.where(step >= packed, step - packed, step))
+        spots.append((entry, second))
         there = gi * rows_l + lr
         level = jnp.where((there >= 0) & (there < rows_l * halves), 0.0, -1e30).astype(F32)
         bias = jnp.where(key_lane // cols == d + REACH, level, bias)
@@ -418,8 +430,11 @@
     tail = [jnp.zeros((ch, span - window * cols), F32)] if span > window * cols else []
     groups, owns = [], []
     for f in range(peers):
-        seen = [near[f, spot].astype(F32) for spot in spots]
-        owns.append(seen[REACH][:, :per])
+        seen = [near[f, entry].astype(F32) for entry, _ in spots]
+        seen = [
+            jnp.where(second, v[:, per:], v[:, :per]) for v, (_, second) in zip(seen, spots)
+        ]
+        owns.append(seen[REACH])
         for b in range(batches):
             groups.append(
                 jnp.concatenate([v[:, b * cols : (b + 1) * cols] for v in seen] + tail, axis=1)
@@ -504,7 +519,6 @@
     var = dot(jnp.ones((16, width), jnp.bfloat16), square, NT)[0:1] * (1.0 / width)
     qkv[...] = dot(gt[...], z.astype(jnp.bfloat16)) * lax.rsqrt(var + 1e-06)
     tiles = peers // pair
-    scale = 1.0 / math.sqrt(HEAD_DIM)
 
     def tile_of(part, h, t):
         top = part * inner + h * HEAD_DIM
@@ -518,7 +532,7 @@
     for h in range(HEADS):
         ks = [turned(tile_of(1, h, t), s) for t, s in shifts]
         for p in range(tiles):
-            q = tile_of(0, h, p) * scale
+            q = tile_of(0, h, p)
             for slot, k in zip(logits[p], ks):
                 slot.append(jnp.sum(q * k, axis=0, keepdims=True))
     shares = []
@@ -536,7 +550,7 @@
             )
 
     weight_copies[4].wait()
-    stream = stream1[...] + dot(mixed_t[...].T.astype(jnp.bfloat16), to[...])
+    stream = stream1[...] + dot(mixed_t[...].astype(jnp.bfloat16).T, to[...])
     stream = stream - jnp.mean(stream, axis=-1, keepdims=True)
     share = lax.rsqrt(jnp.mean(stream * stream, axis=-1, keepdims=True) + 1e-06)
     predicted = dot(final_ref[...], (stream * share).astype(jnp.bfloat16), NT)
@@ -621,7 +635,7 @@
             sems((5,)),
             pltpu.VMEM((rows_l, ch, lanes), bf16),
             pltpu.VMEM((rows_l, ch, lanes), F32),
-            pltpu.VMEM((peers, 3 * REACH + 1, ch, lanes), bf16),
+            pltpu.VMEM((peers, REACH + 2, ch, lanes), bf16),
             pltpu.VMEM((peers, ch, lanes), F32),
             pltpu.VMEM((tokens // lanes, 8, lanes), F32),
             pltpu.VMEM((peers, 8, lanes), F32),
@@ -668,7 +682,8 @@
         frames_l == 1
         and rows_l == lax.axis_size("frame")
         and rows_l >= 3 * REACH
-        and 128 % per == 0
+        and 2 * per == 128
+        and REACH == 2
         and (rows_l * per) % 128 == 0
         and ch % 16 == 0
         and batches <= 8

time: 29.4 us -> 27.5 us (0.935)
  Pallas kernels: 27.9 us -> 26 us
    pallas_call x1, Pallas kernels: 27.9 us -> 26 us  [fused(): pl.pallas_call(functools.partial(fused_kernel, peers, halves), out_shape=...]
where the time goes in v4:
time: 27.5 us; the launch traced here: 27.3 us
  Pallas kernels  26 us (95%)
  other arithmetic  1.3 us (5%)
    pallas_call x1, Pallas kernels, fused(): pl.pallas_call(functools.partial(fused_kernel, peers, halves), out_shape=...  26 us
    mul x1, other arithmetic, fused(): return summed * (1.0 / ch)  1.3 us

profile of v4, /device:TPU:0, one launch (start us, length us, event | category | flops | bytes accessed | tf_op | source)
XLA Modules:
  0.0 27.3 jit_solution(6482566206351218996)
XLA Ops:
  0.0 26.0 %shard_map.100 = f32[2,1,8,32]{3,2,1,0:T(8,128)} custom-call(s32[2]{0:T(128)} %times_ref.1, f32[2,1,8,16,32]{4,3,2,1,0:T(8,128)} %bitcast.7, f32[2,1,8,16,32]{4,3,2,1,0:T(8,128)} %bitcast.8, bf16[16,1152]{1,0:T(8,128)(2,1)} %patch_ref.1, bf16[16,1152]{1,0:T(8,128)(2,1)} %bitcast.9, bf16[256,1152]{1,0:T(8,128)(2,1)} %tw_hbm.1, bf16[1728,1152]{1,0:T(8,128)(2,1)} %bitcast.5, ...), custom_call_target="tpu_custom_call" | custom-call | flops 4000000000 | bytes 11000000 | tf_op jit(solution)/shard_map/pallas_call | solution.py:624
  26.0 1.3 %broadcast_multiply_fusion = f32[2,1,8,32]{3,2,1,0:T(8,128)} fusion(f32[2,1,8,32]{3,2,1,0:T(8,128)} %shard_map.100), kind=kLoop, calls=%fused_computation | loop fusion | flops 512 | bytes 4096 | tf_op jit(solution)/shard_map/mul | solution.py:675

commit v5 on v4

--- a/solution.py
+++ b/solution.py
@@ -329,8 +329,6 @@
     for k in range(1, peers):
         x_copy(lax.rem(fi + k, peers)).start()
     halos(lambda copy: copy.start())
-    for k in range(1, peers):
-        t_copy(lax.rem(fi + k, peers)).start()
     near[fi, 0:packed] = x_ref[pl.ds(start_of(fi), packed)]
     goal[fi] = target_ref[fi]
     takes_halo = ((fi < REACH) & (gi > 0)) | ((fi >= peers - REACH) & (gi < halves - 1))
@@ -381,6 +379,8 @@
     ).astype(jnp.bfloat16)
     small = dot(base_c, base_c, NT, HI) * (1.0 / width)
     small = jnp.concatenate(pieces(small, 3), axis=0)
+    for k in range(1, peers):
+        t_copy(lax.rem(fi + k, peers)).start()
     weight_copies[3].wait()
     turned_full = dot(tp[...], full[...], NT)
     scale = 1.0 / math.sqrt(HEAD_DIM)
@@ -513,11 +513,12 @@
         )
 
     z = state[...]
-    stream1[...] = dot(z.T.astype(jnp.bfloat16), full[...])
+    z = z.astype(jnp.bfloat16)
+    stream1[...] = dot(z.T, full[...])
     square = stream1[...]
     square = (square * square).astype(jnp.bfloat16)
     var = dot(jnp.ones((16, width), jnp.bfloat16), square, NT)[0:1] * (1.0 / width)
-    qkv[...] = dot(gt[...], z.astype(jnp.bfloat16)) * lax.rsqrt(var + 1e-06)
+    qkv[...] = dot(gt[...], z) * lax.rsqrt(var + 1e-06)
     tiles = peers // pair
 
     def tile_of(part, h, t):

time: 27.5 us -> 27.4 us (level)
  no operation moved by 1% of the time
where the time goes in v5:
time: 27.4 us; the launch traced here: 27.2 us
  Pallas kernels  25.9 us (95%)
  other arithmetic  1.3 us (5%)
    pallas_call x1, Pallas kernels, fused(): pl.pallas_call(functools.partial(fused_kernel, peers, halves), out_shape=...  25.9 us
    mul x1, other arithmetic, fused(): return summed * (1.0 / ch)  1.3 us

profile of v5, /device:TPU:0, one launch (start us, length us, event | category | flops | bytes accessed | tf_op | source)
XLA Modules:
  0.0 27.2 jit_solution(15100670742222772901)
XLA Ops:
  0.0 25.9 %shard_map.100 = f32[2,1,8,32]{3,2,1,0:T(8,128)} custom-call(s32[2]{0:T(128)} %times_ref.1, f32[2,1,8,16,32]{4,3,2,1,0:T(8,128)} %bitcast.7, f32[2,1,8,16,32]{4,3,2,1,0:T(8,128)} %bitcast.8, bf16[16,1152]{1,0:T(8,128)(2,1)} %patch_ref.1, bf16[16,1152]{1,0:T(8,128)(2,1)} %bitcast.9, bf16[256,1152]{1,0:T(8,128)(2,1)} %tw_hbm.1, bf16[1728,1152]{1,0:T(8,128)(2,1)} %bitcast.5, ...), custom_call_target="tpu_custom_call" | custom-call | flops 4000000000 | bytes 11000000 | tf_op jit(solution)/shard_map/pallas_call | solution.py:625
  25.9 1.3 %broadcast_multiply_fusion = f32[2,1,8,32]{3,2,1,0:T(8,128)} fusion(f32[2,1,8,32]{3,2,1,0:T(8,128)} %shard_map.100), kind=kLoop, calls=%fused_computation | loop fusion | flops 512 | bytes 4096 | tf_op jit(solution)/shard_map/mul | solution.py:676
